TPU v7x, 32 devices: a whole 2x2x4 slice. The times are simulated.
32 devices in a mesh: dp: 4 (over y, core), mp: 8 (over z, x).
Axes of the slice: x: 2, y: 2, z: 4, core: 2. Of those that a mesh axis runs over, the one named last changes fastest.
Arguments:
- acts: bfloat16 [512, 8192], P('mp', 'dp'), may hold values from -6 to 6
- grads: bfloat16 [512, 28672], P('dp', 'mp'), may hold values from -6 to 6
- query_acts: bfloat16 [256, 8192], P('mp', 'dp'), may hold values from -6 to 6
- query_grads: bfloat16 [256, 28672], P('dp', 'mp'), may hold values from -6 to 6
- basis_in: bfloat16 [8192, 8192], P('dp', 'mp'), may hold values from -0.0625 to 0.0625
- basis_out: bfloat16 [28672, 14336], P('mp', 'dp'), may hold values from -0.03125 to 0.03125
Outputs:
- eigenvalues: float32 [8192, 14336], P('mp', 'dp')
- scores: float32 [16, 512], replicated
All inputs are finite; a program needn't handle non-finite values.
Results may differ from a plain program's by a relative error of at most 0.0047.
Values may be sent and summed in bfloat16 or wider, within the bound.
A program may use at most 128 MiB of HBM per device.

v0:
```python
import math

import jax
import jax.numpy as jnp
from jax import lax
from jax.sharding import PartitionSpec as P

D = 8192
K = 14336
QTOK = 16


def split_rows(joined, groups, first):
    width = joined.shape[1]
    shaped = joined.reshape(groups, joined.shape[0] // groups, width)
    return (shaped[:, :first].reshape(-1, width), shaped[:, first:].reshape(-1, width))


def shards(acts, grads, query_acts, query_grads, basis_in, basis_out):
    n_model = lax.axis_size("mp")
    n_data = lax.axis_size("dp")
    rows_in = jnp.concatenate([acts, query_acts], axis=0)
    rows_out = jnp.concatenate([grads, query_grads], axis=0)
    part_in = jnp.dot(
        lax.all_gather(rows_in, "mp", axis=0, tiled=True),
        basis_in,
        preferred_element_type=jnp.float32,
    )
    part_out = jnp.dot(
        lax.all_gather(rows_out, "dp", axis=0, tiled=True),
        basis_out,
        preferred_element_type=jnp.float32,
    )
    rot_in = lax.psum(part_in, "dp").astype(jnp.bfloat16)
    rot_out = lax.psum(part_out, "mp").astype(jnp.bfloat16)
    tok_in, qry_in = split_rows(rot_in, n_model, acts.shape[0])
    tok_out, qry_out = split_rows(rot_out, n_data, grads.shape[0])
    count = tok_in.shape[0]
    sq_in = (tok_in.astype(jnp.float32) ** 2).astype(jnp.bfloat16)
    sq_out = (tok_out.astype(jnp.float32) ** 2).astype(jnp.bfloat16)
    contract_rows = (((0,), (0,)), ((), ()))
    eigenvalues = (
        lax.dot_general(sq_in, sq_out, contract_rows, preferred_element_type=jnp.float32) / count
    )
    queries = qry_in.shape[0] // QTOK
    qa_blocks = qry_in.reshape(queries, QTOK, qry_in.shape[1])
    qg_blocks = qry_out.reshape(queries, QTOK, qry_out.shape[1])

    def one_query(carry, pair):
        left, right = pair
        rotated = (
            lax.dot_general(left, right, contract_rows, preferred_element_type=jnp.float32) / QTOK
        )
        precond = (rotated / (eigenvalues + 0.1)).astype(jnp.bfloat16)
        mapped = jnp.dot(tok_in, precond, preferred_element_type=jnp.float32)
        return (carry, jnp.sum(mapped * tok_out, axis=1))

    unused, partial_scores = lax.scan(one_query, jnp.zeros((), jnp.float32), (qa_blocks, qg_blocks))
    scores = lax.psum(partial_scores, ("dp", "mp")) * math.sqrt(QTOK / (D * K))
    return (eigenvalues, scores)


def solution(mesh):
    placed = (
        P("mp", "dp"),
        P("dp", "mp"),
        P("mp", "dp"),
        P("dp", "mp"),
        P("dp", "mp"),
        P("mp", "dp"),
    )
    return jax.shard_map(
        shards, mesh=mesh, in_specs=placed, out_specs=(P("mp", "dp"), P()), check_vma=False
    )
```

profile of v0, /device:TPU:0, one launch (start us, length us, event | category | flops | bytes accessed | tf_op | source)
XLA Modules:
  0.0 868.0 jit_solution(3731041896051231189)
XLA Ops:
  7.2 0.0 all-gather.3.cloned.1.call-start
  7.2 1.8 pad_maximum_fusion.1
  9.0 0.0 all-gather.3.cloned.1.call-update
  9.0 0.0 all-gather.5.cloned.1.call-start
  9.1 2.6 pad_maximum_fusion
  11.7 0.0 all-gather.5.cloned.1.call-update
  11.7 62.2 %all-gather.3.cloned.1.call-done = bf16[768,2048]{1,0:T(8,128)(2,1)} async-done(((bf16[96,2048]{1,0:T(8,128)(2,1)}), bf16[768,2048]{1,0:T(8,128)(2,1)}) %all-gather.3.cloned.1.call-update) | async-done | bytes 3145744 | tf_op jit(solution)/shard_map/all_gather | solution.py:25
  73.9 8.2 fusion.13
  82.2 83.9 %all-reduce.2 = bf16[768,1024]{1,0:T(8,128)(2,1)S(1)} all-reduce(f32[768,1024]{1,0:T(8,128)} %fusion.13), channel_id=1, replica_groups=mesh['dp'=4,'mp'=8] {'dp'}, use_global_device_ids=true, to_apply=%region_0.0 | all-reduce | flops 786432 | bytes 4718592 | tf_op jit(solution)/shard_map/psum | solution.py:34
  166.1 1.1 slice.16
  167.2 0.2 multiply_convert_fusion.1
  167.4 0.0 all-gather.5.cloned.1.call-done
  167.4 29.0 %fusion.14 = f32[768,3584]{1,0:T(8,128)} fusion(bf16[768,3584]{1,0:T(8,128)(2,1)} %all-gather.5.cloned.1.call-done, bf16[3584,3584]{1,0:T(8,128)(2,1)} %param.13), kind=kOutput, calls=%fused_computation.17 | convolution fusion | flops 19730006016 | bytes 42205184 | tf_op jit(solution)/shard_map/dot_general | solution.py:29
  196.4 426.2 %all-reduce.3 = bf16[768,3584]{1,0:T(8,128)(2,1)} all-reduce(f32[768,3584]{1,0:T(8,128)} %fusion.14), channel_id=1, replica_groups=mesh['dp'=4,'mp'=8] {'mp'}, use_global_device_ids=true, to_apply=%region_1.0 | all-reduce | flops 2752512 | bytes 16515072 | tf_op jit(solution)/shard_map/psum | solution.py:35
  622.6 2.9 slice.19
  625.5 0.0 copy-start
  625.5 4.7 multiply_convert_fusion
  630.1 0.0 copy-done
  630.2 2.1 slice.17
  632.2 5.9 copy.9
  638.1 0.0 copy-start.1
  638.1 9.7 %convolution_multiply_fusion = f32[1024,3584]{1,0:T(8,128)} fusion(bf16[512,1024]{1,0:T(8,128)(2,1)S(1)} %bitcast.46, bf16[512,3584]{1,0:T(8,128)(2,1)} %bitcast.41), kind=kOutput, calls=%fused_computation.10 | convolution fusion | flops 3761766400 | bytes 19398656 | tf_op jit(solution)/shard_map/dot_general | solution.py:43
  647.8 0.0 copy-done.1
  647.8 173.8 %while.10 = (s32[]{:T(128)}, f32[16,512]{1,0:T(8,128)S(1)}, bf16[16,16,1024]{2,1,0:T(8,128)(2,1)S(1)}, bf16[16,16,3584]{2,1,0:T(8,128)(2,1)}, f32[1024,3584]{1,0...) while((s32[]{:T(128)}, f32[16,512]{1,0:T(8,128)S(1)}, ...), condition=%wide.region_4.5_spmd, body=%wide.region_2.4_spmd.sunk | while | flops 3895721472 | bytes 19553384 | solution.py:58
  647.8 10.8 %fusion.29 = f32[512]{0:T(512)S(1)} fusion(bf16[512,3584]{0,1:T(8,128)(2,1)} %get-tuple-element.121, bf16[512,1024]{1,0:T(8,128)(2,1)S(1)} %get-tuple-element.120, f32[1024,3584]{1,0:T(8,128)} %get-tuple-element.119, bf16[16,16,3584]{2,1,0:T(8,128)(2,1)} %get-tuple-element.118, s32[]{:T(128)S(6)} %copy.15, ...), kind=kOutput, calls=%fused_computation.2.clone.1 | convolution fusion | flops 3895721472 | bytes 19549184 | tf_op jit(solution)/shard_map/while/body/eval_jaxpr/dot_general | solution.py:55
  658.6 0.1 dynamic_update_slice.5
  658.7 10.8 %fusion.29 = f32[512]{0:T(512)S(1)} fusion(bf16[512,3584]{0,1:T(8,128)(2,1)} %get-tuple-element.121, bf16[512,1024]{1,0:T(8,128)(2,1)S(1)} %get-tuple-element.120, f32[1024,3584]{1,0:T(8,128)} %get-tuple-element.119, bf16[16,16,3584]{2,1,0:T(8,128)(2,1)} %get-tuple-element.118, s32[]{:T(128)S(6)} %copy.15, ...), kind=kOutput, calls=%fused_computation.2.clone.1 | convolution fusion | flops 3895721472 | bytes 19549184 | tf_op jit(solution)/shard_map/while/body/eval_jaxpr/dot_general | solution.py:55
  669.5 0.1 dynamic_update_slice.5
  669.6 10.8 %fusion.29 = f32[512]{0:T(512)S(1)} fusion(bf16[512,3584]{0,1:T(8,128)(2,1)} %get-tuple-element.121, bf16[512,1024]{1,0:T(8,128)(2,1)S(1)} %get-tuple-element.120, f32[1024,3584]{1,0:T(8,128)} %get-tuple-element.119, bf16[16,16,3584]{2,1,0:T(8,128)(2,1)} %get-tuple-element.118, s32[]{:T(128)S(6)} %copy.15, ...), kind=kOutput, calls=%fused_computation.2.clone.1 | convolution fusion | flops 3895721472 | bytes 19549184 | tf_op jit(solution)/shard_map/while/body/eval_jaxpr/dot_general | solution.py:55
  680.3 0.1 dynamic_update_slice.5
  680.4 10.8 %fusion.29 = f32[512]{0:T(512)S(1)} fusion(bf16[512,3584]{0,1:T(8,128)(2,1)} %get-tuple-element.121, bf16[512,1024]{1,0:T(8,128)(2,1)S(1)} %get-tuple-element.120, f32[1024,3584]{1,0:T(8,128)} %get-tuple-element.119, bf16[16,16,3584]{2,1,0:T(8,128)(2,1)} %get-tuple-element.118, s32[]{:T(128)S(6)} %copy.15, ...), kind=kOutput, calls=%fused_computation.2.clone.1 | convolution fusion | flops 3895721472 | bytes 19549184 | tf_op jit(solution)/shard_map/while/body/eval_jaxpr/dot_general | solution.py:55
  691.2 0.1 dynamic_update_slice.5
  691.3 10.8 %fusion.29 = f32[512]{0:T(512)S(1)} fusion(bf16[512,3584]{0,1:T(8,128)(2,1)} %get-tuple-element.121, bf16[512,1024]{1,0:T(8,128)(2,1)S(1)} %get-tuple-element.120, f32[1024,3584]{1,0:T(8,128)} %get-tuple-element.119, bf16[16,16,3584]{2,1,0:T(8,128)(2,1)} %get-tuple-element.118, s32[]{:T(128)S(6)} %copy.15, ...), kind=kOutput, calls=%fused_computation.2.clone.1 | convolution fusion | flops 3895721472 | bytes 19549184 | tf_op jit(solution)/shard_map/while/body/eval_jaxpr/dot_general | solution.py:55
  702.1 0.1 dynamic_update_slice.5
  702.1 10.8 %fusion.29 = f32[512]{0:T(512)S(1)} fusion(bf16[512,3584]{0,1:T(8,128)(2,1)} %get-tuple-element.121, bf16[512,1024]{1,0:T(8,128)(2,1)S(1)} %get-tuple-element.120, f32[1024,3584]{1,0:T(8,128)} %get-tuple-element.119, bf16[16,16,3584]{2,1,0:T(8,128)(2,1)} %get-tuple-element.118, s32[]{:T(128)S(6)} %copy.15, ...), kind=kOutput, calls=%fused_computation.2.clone.1 | convolution fusion | flops 3895721472 | bytes 19549184 | tf_op jit(solution)/shard_map/while/body/eval_jaxpr/dot_general | solution.py:55
  712.9 0.1 dynamic_update_slice.5
  713.0 10.8 %fusion.29 = f32[512]{0:T(512)S(1)} fusion(bf16[512,3584]{0,1:T(8,128)(2,1)} %get-tuple-element.121, bf16[512,1024]{1,0:T(8,128)(2,1)S(1)} %get-tuple-element.120, f32[1024,3584]{1,0:T(8,128)} %get-tuple-element.119, bf16[16,16,3584]{2,1,0:T(8,128)(2,1)} %get-tuple-element.118, s32[]{:T(128)S(6)} %copy.15, ...), kind=kOutput, calls=%fused_computation.2.clone.1 | convolution fusion | flops 3895721472 | bytes 19549184 | tf_op jit(solution)/shard_map/while/body/eval_jaxpr/dot_general | solution.py:55
  723.8 0.1 dynamic_update_slice.5
  723.9 10.8 %fusion.29 = f32[512]{0:T(512)S(1)} fusion(bf16[512,3584]{0,1:T(8,128)(2,1)} %get-tuple-element.121, bf16[512,1024]{1,0:T(8,128)(2,1)S(1)} %get-tuple-element.120, f32[1024,3584]{1,0:T(8,128)} %get-tuple-element.119, bf16[16,16,3584]{2,1,0:T(8,128)(2,1)} %get-tuple-element.118, s32[]{:T(128)S(6)} %copy.15, ...), kind=kOutput, calls=%fused_computation.2.clone.1 | convolution fusion | flops 3895721472 | bytes 19549184 | tf_op jit(solution)/shard_map/while/body/eval_jaxpr/dot_general | solution.py:55
  734.6 0.1 dynamic_update_slice.5
  734.7 10.8 %fusion.29 = f32[512]{0:T(512)S(1)} fusion(bf16[512,3584]{0,1:T(8,128)(2,1)} %get-tuple-element.121, bf16[512,1024]{1,0:T(8,128)(2,1)S(1)} %get-tuple-element.120, f32[1024,3584]{1,0:T(8,128)} %get-tuple-element.119, bf16[16,16,3584]{2,1,0:T(8,128)(2,1)} %get-tuple-element.118, s32[]{:T(128)S(6)} %copy.15, ...), kind=kOutput, calls=%fused_computation.2.clone.1 | convolution fusion | flops 3895721472 | bytes 19549184 | tf_op jit(solution)/shard_map/while/body/eval_jaxpr/dot_general | solution.py:55
  745.5 0.1 dynamic_update_slice.5
  745.6 10.8 %fusion.29 = f32[512]{0:T(512)S(1)} fusion(bf16[512,3584]{0,1:T(8,128)(2,1)} %get-tuple-element.121, bf16[512,1024]{1,0:T(8,128)(2,1)S(1)} %get-tuple-element.120, f32[1024,3584]{1,0:T(8,128)} %get-tuple-element.119, bf16[16,16,3584]{2,1,0:T(8,128)(2,1)} %get-tuple-element.118, s32[]{:T(128)S(6)} %copy.15, ...), kind=kOutput, calls=%fused_computation.2.clone.1 | convolution fusion | flops 3895721472 | bytes 19549184 | tf_op jit(solution)/shard_map/while/body/eval_jaxpr/dot_general | solution.py:55
  756.4 0.1 dynamic_update_slice.5
  756.5 10.8 %fusion.29 = f32[512]{0:T(512)S(1)} fusion(bf16[512,3584]{0,1:T(8,128)(2,1)} %get-tuple-element.121, bf16[512,1024]{1,0:T(8,128)(2,1)S(1)} %get-tuple-element.120, f32[1024,3584]{1,0:T(8,128)} %get-tuple-element.119, bf16[16,16,3584]{2,1,0:T(8,128)(2,1)} %get-tuple-element.118, s32[]{:T(128)S(6)} %copy.15, ...), kind=kOutput, calls=%fused_computation.2.clone.1 | convolution fusion | flops 3895721472 | bytes 19549184 | tf_op jit(solution)/shard_map/while/body/eval_jaxpr/dot_general | solution.py:55
  767.2 0.1 dynamic_update_slice.5
  767.3 10.8 %fusion.29 = f32[512]{0:T(512)S(1)} fusion(bf16[512,3584]{0,1:T(8,128)(2,1)} %get-tuple-element.121, bf16[512,1024]{1,0:T(8,128)(2,1)S(1)} %get-tuple-element.120, f32[1024,3584]{1,0:T(8,128)} %get-tuple-element.119, bf16[16,16,3584]{2,1,0:T(8,128)(2,1)} %get-tuple-element.118, s32[]{:T(128)S(6)} %copy.15, ...), kind=kOutput, calls=%fused_computation.2.clone.1 | convolution fusion | flops 3895721472 | bytes 19549184 | tf_op jit(solution)/shard_map/while/body/eval_jaxpr/dot_general | solution.py:55
  778.1 0.1 dynamic_update_slice.5
  778.2 10.8 %fusion.29 = f32[512]{0:T(512)S(1)} fusion(bf16[512,3584]{0,1:T(8,128)(2,1)} %get-tuple-element.121, bf16[512,1024]{1,0:T(8,128)(2,1)S(1)} %get-tuple-element.120, f32[1024,3584]{1,0:T(8,128)} %get-tuple-element.119, bf16[16,16,3584]{2,1,0:T(8,128)(2,1)} %get-tuple-element.118, s32[]{:T(128)S(6)} %copy.15, ...), kind=kOutput, calls=%fused_computation.2.clone.1 | convolution fusion | flops 3895721472 | bytes 19549184 | tf_op jit(solution)/shard_map/while/body/eval_jaxpr/dot_general | solution.py:55
  789.0 0.1 dynamic_update_slice.5
  789.0 10.8 %fusion.29 = f32[512]{0:T(512)S(1)} fusion(bf16[512,3584]{0,1:T(8,128)(2,1)} %get-tuple-element.121, bf16[512,1024]{1,0:T(8,128)(2,1)S(1)} %get-tuple-element.120, f32[1024,3584]{1,0:T(8,128)} %get-tuple-element.119, bf16[16,16,3584]{2,1,0:T(8,128)(2,1)} %get-tuple-element.118, s32[]{:T(128)S(6)} %copy.15, ...), kind=kOutput, calls=%fused_computation.2.clone.1 | convolution fusion | flops 3895721472 | bytes 19549184 | tf_op jit(solution)/shard_map/while/body/eval_jaxpr/dot_general | solution.py:55
  799.8 0.1 dynamic_update_slice.5
  799.9 10.8 %fusion.29 = f32[512]{0:T(512)S(1)} fusion(bf16[512,3584]{0,1:T(8,128)(2,1)} %get-tuple-element.121, bf16[512,1024]{1,0:T(8,128)(2,1)S(1)} %get-tuple-element.120, f32[1024,3584]{1,0:T(8,128)} %get-tuple-element.119, bf16[16,16,3584]{2,1,0:T(8,128)(2,1)} %get-tuple-element.118, s32[]{:T(128)S(6)} %copy.15, ...), kind=kOutput, calls=%fused_computation.2.clone.1 | convolution fusion | flops 3895721472 | bytes 19549184 | tf_op jit(solution)/shard_map/while/body/eval_jaxpr/dot_general | solution.py:55
  810.7 0.1 dynamic_update_slice.5
  810.8 10.8 %fusion.29 = f32[512]{0:T(512)S(1)} fusion(bf16[512,3584]{0,1:T(8,128)(2,1)} %get-tuple-element.121, bf16[512,1024]{1,0:T(8,128)(2,1)S(1)} %get-tuple-element.120, f32[1024,3584]{1,0:T(8,128)} %get-tuple-element.119, bf16[16,16,3584]{2,1,0:T(8,128)(2,1)} %get-tuple-element.118, s32[]{:T(128)S(6)} %copy.15, ...), kind=kOutput, calls=%fused_computation.2.clone.1 | convolution fusion | flops 3895721472 | bytes 19549184 | tf_op jit(solution)/shard_map/while/body/eval_jaxpr/dot_general | solution.py:55
  821.6 0.1 dynamic_update_slice.5
  821.6 38.9 %psum.23 = f32[16,512]{1,0:T(8,128)S(1)} all-reduce(f32[16,512]{1,0:T(8,128)S(1)} %get-tuple-element.39), channel_id=1, replica_groups=mesh['dp'=4,'mp'=8] {'dp','mp'}, use_global_device_ids=true, to_apply=%region_5.6 | all-reduce | flops 8192 | bytes 65536 | tf_op jit(solution)/shard_map/psum | solution.py:59
  860.6 0.6 broadcast_multiply_fusion
  (2 shorter events, 0.0 us)
Async XLA Ops:
  7.2 66.8 %all-gather.3.cloned.1.call-start = ((), (), s32[]{:S(2)}) async-start(), calls=%async_computation | async-start | bytes 3538944 | tf_op jit(solution)/shard_map/all_gather | solution.py:25
  9.0 158.4 %all-gather.5.cloned.1.call-start = ((), (), s32[]{:S(2)}) async-start(), calls=%async_computation.1 | async-start | bytes 6881280 | tf_op jit(solution)/shard_map/all_gather | solution.py:30
  625.5 4.7 copy-start
  638.1 9.7 %copy-start.1 = (bf16[8,64,1024]{2,1,0:T(8,128)(2,1)S(1)}, bf16[8,64,1024]{2,1,0:T(8,128)(2,1)}, u32[]{:S(2)}) copy-start(bf16[8,64,1024]{2,1,0:T(8,128)(2,1)} %slice.16) | copy-start | bytes 3145732
Sparse Core Ops, SparseCore 0:
  10.8 63.1 all-gather.2
  75.5 65.8 all-gather.4
where the time goes:
time: 869 us; the launch traced here: 868 us
  blocking collectives  549 us (63%)
  matrix products  219 us (25%)
  waiting for transfers between devices  62.3 us (7%)
  between operations  14.1 us (2%)
  local copies, waits for them, and re-layouts  13 us (1%)
  other arithmetic  9.89 us (1%)
    psum x1, blocking collectives, shards(): rot_out = lax.psum(part_out, 'mp').astype(jnp.bfloat16)  426 us
    dot_general x16, matrix products, one_query(): mapped = jnp.dot(tok_in, precond, preferred_element_type=jnp.float32)  172 us
    psum x1, blocking collectives, shards(): rot_in = lax.psum(part_in, 'dp').astype(jnp.bfloat16)  83.9 us
    all_gather x1, waiting for transfers between devices, shards(): lax.all_gather(rows_in, 'mp', axis=0, tiled=True)  62.2 us
    psum x1, blocking collectives, shards(): scores = lax.psum(partial_scores, ('dp', 'mp')) * math.sqrt(QTOK / (D * K))  38.9 us
    dot_general x1, matrix products, shards(): jnp.dot(lax.all_gather(rows_out, 'dp', axis=0, tiled=True), basis_out, pr...  29 us
  transfers between devices with their start and end apart: 2, of which 1 were waited for; matrix products, arithmetic and copies ran while one was open for 1% of the time, Pallas kernels for 0%

commit v1 on v0

--- a/solution.py
+++ b/solution.py
@@ -1,13 +1,425 @@
+import functools
 import math
 
 import jax
 import jax.numpy as jnp
 from jax import lax
+from jax.experimental import pallas as pl
+from jax.experimental.pallas import tpu as pltpu
 from jax.sharding import PartitionSpec as P
 
-D = 8192
-K = 14336
 QTOK = 16
+F32 = jnp.float32
+BF16 = jnp.bfloat16
+MESH = pl.DeviceIdType.MESH
+
+
+def bit(v, b):
+    return (v // 2**b) % 2
+
+
+def reverse_bits(v, k):
+    return sum(bit(v, b) * 2 ** (k - 1 - b) for b in range(k))
+
+
+def log2(n):
+    return n.bit_length() - 1
+
+
+def kernel(cfg, *refs):
+    n_mp, n_dp, chunks = cfg
+    k_mp, k_dp = log2(n_mp), log2(n_dp)
+    (
+        acts, q_acts, grads, q_grads, basis_in, basis_out, eig_out, scores_out,
+        gin, gout, bin_v, bout_v, acc, send_rs, recv_rs, rot_out, acc_in, recv_in, rot_in,
+        act_t, sq_act_t, qact_t, grad_t, sq_grad, qgrad, inverse, eig_v, part, part_in,
+        load_sem, bout_sem, eig_sem, gin_s, gin_r, gout_s, gout_r,
+        rs_s, rs_r, ag_s, ag_r, irs_s, irs_r, iag_s, iag_r, ps_s, ps_r,
+    ) = refs
+    dp, mp = lax.axis_index("dp"), lax.axis_index("mp")
+    pos_m, pos_d = reverse_bits(mp, k_mp), reverse_bits(dp, k_dp)
+    tok_m, qry_m = acts.shape[0], q_acts.shape[0]
+    tok_d, qry_d = grads.shape[0], q_grads.shape[0]
+    row_m, row_d = tok_m + qry_m, tok_d + qry_d
+    rows = row_m * n_mp
+    tokens, queries = tok_m * n_mp, qry_m * n_mp // QTOK
+    width_i = basis_in.shape[1]
+    cw = basis_out.shape[1] // chunks
+    ti = 256
+
+    def along_mp(b):
+        return (dp, mp + (1 - 2 * bit(mp, b)) * 2**b)
+
+    def along_dp(b):
+        return (dp + (1 - 2 * bit(dp, b)) * 2**b, mp)
+
+    def remote(src, dst, s, r, to):
+        return pltpu.make_async_remote_copy(
+            src_ref=src, dst_ref=dst, send_sem=s, recv_sem=r, device_id=to, device_id_type=MESH
+        )
+
+    def rows_at(start, size):
+        return pl.ds(pl.multiple_of(start, 16), size)
+
+    def split_start(me, k, step):
+        size = rows // 2**step
+        return sum(bit(me, b) * (rows // 2 ** (b + 1)) for b in range(step)), size
+
+    barrier = pltpu.get_barrier_semaphore()
+    for b in range(k_mp):
+        pl.semaphore_signal(barrier, inc=1, device_id=along_mp(b), device_id_type=MESH)
+    for b in range(k_dp):
+        pl.semaphore_signal(barrier, inc=1, device_id=along_dp(b), device_id_type=MESH)
+
+    def load_chunk(c):
+        columns = pl.ds(pl.multiple_of(c * cw, 128), cw)
+        return pltpu.make_async_copy(
+            basis_out.at[:, columns], bout_v.at[lax.rem(c, 2)], bout_sem.at[c]
+        )
+
+    loads = [
+        pltpu.make_async_copy(grads, gout.at[rows_at(pos_d * row_d, tok_d)], load_sem.at[0]),
+        pltpu.make_async_copy(
+            q_grads, gout.at[rows_at(pos_d * row_d + tok_d, qry_d)], load_sem.at[1]
+        ),
+        pltpu.make_async_copy(acts, gin.at[rows_at(pos_m * row_m, tok_m)], load_sem.at[2]),
+        pltpu.make_async_copy(
+            q_acts, gin.at[rows_at(pos_m * row_m + tok_m, qry_m)], load_sem.at[3]
+        ),
+    ]
+    load_bin = pltpu.make_async_copy(basis_in, bin_v, load_sem.at[4])
+    for copy in loads:
+        copy.start()
+    load_chunk(0).start()
+    load_chunk(1).start()
+    load_bin.start()
+    pl.semaphore_wait(barrier, k_mp + k_dp)
+
+    def gather_step(buf, me, pos, k, per, step, s, r, along):
+        block = rows_at((pos // 2**step) * 2**step * per, per * 2**step)
+        return remote(buf.at[block], buf.at[block], s.at[step], r.at[step], along(k - 1 - step))
+
+    gin_steps = [
+        gather_step(gin, mp, pos_m, k_mp, row_m, s, gin_s, gin_r, along_mp) for s in range(k_mp)
+    ]
+    gout_steps = [
+        gather_step(gout, dp, pos_d, k_dp, row_d, s, gout_s, gout_r, along_dp) for s in range(k_dp)
+    ]
+    loads[0].wait()
+    loads[1].wait()
+    gout_steps[0].start()
+    loads[2].wait()
+    loads[3].wait()
+    gin_steps[0].start()
+    for s in range(1, k_mp):
+        gin_steps[s - 1].wait_recv()
+        gin_steps[s].start()
+    for s in range(1, k_dp):
+        gout_steps[s - 1].wait_recv()
+        gout_steps[s].start()
+    gout_steps[k_dp - 1].wait_recv()
+    part[0] = jnp.zeros_like(part[0])
+
+    rs_at, offset = [], 0
+    for s in range(k_mp):
+        rs_at.append(offset)
+        offset += rows // 2 ** (s + 1)
+    irs_at, offset = [], 0
+    for s in range(k_dp):
+        irs_at.append(offset)
+        offset += rows // 2 ** (s + 1)
+
+    def rs_copy(s, c):
+        size = rows // 2 ** (s + 1)
+        slot = pl.ds(rs_at[s], size)
+        return remote(
+            send_rs.at[c, slot], recv_rs.at[c, slot], rs_s.at[s, c], rs_r.at[s, c], along_mp(s)
+        )
+
+    def ag_copy(s, c):
+        start, size = split_start(mp, k_mp, k_mp - s)
+        block = rows_at(start, size)
+        return remote(
+            rot_out.at[c, block], rot_out.at[c, block], ag_s.at[s, c], ag_r.at[s, c],
+            along_mp(k_mp - 1 - s),
+        )
+
+    def irs_copy(s):
+        start, size = split_start(dp, k_dp, s)
+        half = size // 2
+        src = rows_at(start + (1 - bit(dp, s)) * half, half)
+        return remote(
+            acc_in.at[src], recv_in.at[pl.ds(irs_at[s], half)], irs_s.at[s], irs_r.at[s], along_dp(s)
+        )
+
+    def iag_copy(s):
+        start, size = split_start(dp, k_dp, k_dp - s)
+        block = rows_at(start, size)
+        return remote(
+            rot_in.at[block], rot_in.at[block], iag_s.at[s], iag_r.at[s], along_dp(k_dp - 1 - s)
+        )
+
+    half = rows // 2
+
+    def rotate_out(c):
+        load_chunk(c).wait()
+        slot, ring = lax.rem(c, 2), lax.rem(c, k_mp + 1)
+        theirs = rows_at((1 - bit(mp, 0)) * half, half)
+        mine = rows_at(bit(mp, 0) * half, half)
+        tile = 256
+
+        @pl.loop(0, cw // tile)
+        def _(j):
+            columns = pl.ds(pl.multiple_of(j * tile, tile), tile)
+            out = jnp.dot(gout[theirs, :], bout_v[slot, :, columns], preferred_element_type=F32)
+            send_rs[c, pl.ds(0, half), columns] = out.astype(BF16)
+
+        rs_copy(0, c).start()
+
+        @pl.loop(0, cw // tile)
+        def _(j):
+            columns = pl.ds(pl.multiple_of(j * tile, tile), tile)
+            acc[ring, :, columns] = jnp.dot(
+                gout[mine, :], bout_v[slot, :, columns], preferred_element_type=F32
+            )
+
+        @pl.when(c + 2 < chunks)
+        def _():
+            load_chunk(c + 2).start()
+
+    def reduce_out(s, c):
+        rs_copy(s - 1, c).wait_recv()
+        ring = lax.rem(c, k_mp + 1)
+        start, size = split_start(mp, k_mp, s)
+        start = start - bit(mp, 0) * half
+        if s == k_mp:
+            total = acc[ring, rows_at(start, size), :] + recv_rs[
+                c, pl.ds(rs_at[s - 1], size), :
+            ].astype(F32)
+            begin, _ = split_start(mp, k_mp, k_mp)
+            rot_out[c, rows_at(begin, size), :] = total.astype(BF16)
+            ag_copy(0, c).start()
+            return
+        part_size = size // 2
+        theirs, mine = (1 - bit(mp, s)) * part_size, bit(mp, s) * part_size
+        base = rs_at[s - 1]
+        send_rs[c, pl.ds(rs_at[s], part_size), :] = (
+            acc[ring, rows_at(start + theirs, part_size), :]
+            + recv_rs[c, rows_at(base + theirs, part_size), :].astype(F32)
+        ).astype(BF16)
+        rs_copy(s, c).start()
+        acc[ring, rows_at(start + mine, part_size), :] = acc[
+            ring, rows_at(start + mine, part_size), :
+        ] + recv_rs[c, rows_at(base + mine, part_size), :].astype(F32)
+
+    def spread_out(s, c):
+        ag_copy(s - 1, c).wait_recv()
+        if s < k_mp:
+            ag_copy(s, c).start()
+
+    def rotate_in():
+        gin_steps[k_mp - 1].wait_recv()
+        load_bin.wait()
+
+        @pl.loop(0, width_i // ti)
+        def _(j):
+            columns = pl.ds(pl.multiple_of(j * ti, ti), ti)
+            acc_in[:, columns] = jnp.dot(
+                gin[...], bin_v[:, columns], preferred_element_type=F32
+            )
+
+        irs_copy(0).start()
+
+    def reduce_in(s):
+        irs_copy(s - 1).wait_recv()
+        start, size = split_start(dp, k_dp, s)
+        where = rows_at(start, size)
+        total = acc_in[where, :] + recv_in[pl.ds(irs_at[s - 1], size), :]
+        if s == k_dp:
+            rot_in[where, :] = total.astype(BF16)
+            iag_copy(0).start()
+        else:
+            acc_in[where, :] = total
+            irs_copy(s).start()
+
+    def spread_in(s):
+        iag_copy(s - 1).wait_recv()
+        if s < k_dp:
+            iag_copy(s).start()
+            return
+        order = [reverse_bits(m, k_mp) * row_m for m in range(n_mp)]
+        for i in range(width_i // ti):
+            cols = pl.ds(i * ti, ti)
+            tok = jnp.concatenate([rot_in[pl.ds(p, tok_m), cols] for p in order], axis=0)
+            qry = jnp.concatenate([rot_in[pl.ds(p + tok_m, qry_m), cols] for p in order], axis=0)
+            flipped = tok.astype(F32).T
+            act_t[cols, :] = flipped
+            sq_act_t[cols, :] = (flipped * flipped).astype(BF16)
+            qact_t[cols, :] = qry.astype(F32).T.astype(BF16)
+
+    def eig_copy(c):
+        columns = pl.ds(pl.multiple_of(c * cw, 128), cw)
+        return pltpu.make_async_copy(
+            eig_v.at[lax.rem(c, 2)], eig_out.at[:, columns], eig_sem.at[c]
+        )
+
+    def score(c):
+        @pl.when(c >= 2)
+        def _():
+            eig_copy(c - 2).wait()
+
+        order = [reverse_bits(d, k_dp) * row_d for d in range(n_dp)]
+        for j in range(cw // ti):
+            cols = pl.ds(j * ti, ti)
+            tok = jnp.concatenate([rot_out[c, pl.ds(p, tok_d), cols] for p in order], axis=0)
+            wide = tok.astype(F32)
+            grad_t[cols, :] = wide.T.astype(BF16)
+            sq_grad[:, cols] = (wide * wide).astype(BF16)
+        for d, p in enumerate(order):
+            qgrad[pl.ds(d * qry_d, qry_d), :] = rot_out[c, pl.ds(p + tok_d, qry_d), :]
+        slot = lax.rem(c, 2)
+
+        @pl.loop(0, width_i // ti)
+        def _(i):
+            at = pl.ds(pl.multiple_of(i * ti, ti), ti)
+            eig = jnp.dot(sq_act_t[at, :], sq_grad[...], preferred_element_type=F32) * (
+                1.0 / tokens
+            )
+            eig_v[slot, at, :] = eig
+            inverse[at, :] = (1.0 / QTOK) / (eig + 0.1)
+
+        eig_copy(c).start()
+
+        @pl.loop(0, queries)
+        def _(q):
+            owner = lax.broadcasted_iota(jnp.int32, qgrad.shape, 0) // QTOK
+            right = jnp.where(owner == q, qgrad[...].astype(F32), 0.0).astype(BF16)
+            total = jnp.zeros((1, tokens), F32)
+            for i in range(width_i // ti):
+                at = pl.ds(i * ti, ti)
+                rotated = jnp.dot(qact_t[at, :], right, preferred_element_type=F32)
+                precond = (rotated * inverse[at, :]).astype(BF16)
+                mapped = jnp.dot(precond, grad_t[...], preferred_element_type=F32)
+                total = total + jnp.sum(mapped * act_t[at, :], axis=0, keepdims=True)
+            part[0, pl.ds(q, 1), :] = part[0, pl.ds(q, 1), :] + total
+
+    lag = 2 * k_mp
+
+    @pl.loop(0, chunks + lag)
+    def _(w):
+        @pl.when(w < chunks)
+        def _():
+            rotate_out(w)
+
+        def staged(s, run):
+            @pl.when(jnp.logical_and(w >= s, w < chunks + s))
+            def _():
+                run(w - s)
+
+        for s in range(1, k_mp + 1):
+            staged(s, functools.partial(reduce_out, s))
+        for s in range(1, k_mp):
+            staged(k_mp + s, functools.partial(spread_out, s))
+
+        in_stages = (
+            [rotate_in]
+            + [functools.partial(reduce_in, s) for s in range(1, k_dp + 1)]
+            + [functools.partial(spread_in, s) for s in range(1, k_dp + 1)]
+        )
+        for n, run in enumerate(in_stages):
+            pl.when(w == n + 1)(run)
+
+        staged(lag, functools.partial(spread_out, k_mp))
+        staged(lag, score)
+
+    partners = [along_dp(b) for b in range(k_dp)] + [along_mp(b) for b in range(k_mp)]
+    for n, to in enumerate(partners):
+        copy = remote(part.at[n], part_in.at[n], ps_s.at[n], ps_r.at[n], to)
+        copy.start()
+        copy.wait_recv()
+        part[n + 1] = part[n] + part_in[n]
+        copy.wait_send()
+    scale = math.sqrt(QTOK / (width_i * n_mp * basis_out.shape[1] * n_dp))
+    scores_out[...] = part[len(partners)] * scale
+
+    for copy in gin_steps + gout_steps:
+        copy.wait_send()
+    for s in range(k_dp):
+        irs_copy(s).wait_send()
+        iag_copy(s).wait_send()
+
+    @pl.loop(0, chunks)
+    def _(c):
+        for s in range(k_mp):
+            rs_copy(s, c).wait_send()
+            ag_copy(s, c).wait_send()
+
+    eig_copy(jnp.int32(chunks - 2)).wait()
+    eig_copy(jnp.int32(chunks - 1)).wait()
+
+
+def fused(n_mp, n_dp, chunks, acts, grads, query_acts, query_grads, basis_in, basis_out):
+    k_mp, k_dp = log2(n_mp), log2(n_dp)
+    rows = (acts.shape[0] + query_acts.shape[0]) * n_mp
+    tokens = acts.shape[0] * n_mp
+    queries = query_acts.shape[0] * n_mp
+    depth_in, width_i = basis_in.shape
+    depth_out, width_o = basis_out.shape
+    cw = width_o // chunks
+    moved = rows - rows // n_mp
+    moved_in = rows - rows // n_dp
+    hops = k_mp + k_dp
+    small = (hops, queries // QTOK, tokens)
+    dma = pltpu.SemaphoreType.DMA
+    scratch = [
+        pltpu.VMEM((rows, depth_in), BF16),
+        pltpu.VMEM((rows, depth_out), BF16),
+        pltpu.VMEM((depth_in, width_i), BF16),
+        pltpu.VMEM((2, depth_out, cw), BF16),
+        pltpu.VMEM((k_mp + 1, rows // 2, cw), F32),
+        pltpu.VMEM((chunks, moved, cw), BF16),
+        pltpu.VMEM((chunks, moved, cw), BF16),
+        pltpu.VMEM((chunks, rows, cw), BF16),
+        pltpu.VMEM((rows, width_i), F32),
+        pltpu.VMEM((moved_in, width_i), F32),
+        pltpu.VMEM((rows, width_i), BF16),
+        pltpu.VMEM((width_i, tokens), F32),
+        pltpu.VMEM((width_i, tokens), BF16),
+        pltpu.VMEM((width_i, queries), BF16),
+        pltpu.VMEM((cw, tokens), BF16),
+        pltpu.VMEM((tokens, cw), BF16),
+        pltpu.VMEM((queries, cw), BF16),
+        pltpu.VMEM((width_i, cw), F32),
+        pltpu.VMEM((2, width_i, cw), F32),
+        pltpu.VMEM((hops + 1,) + small[1:], F32),
+        pltpu.VMEM(small, F32),
+        dma((5,)), dma((chunks,)), dma((chunks,)),
+        dma((k_mp,)), dma((k_mp,)), dma((k_dp,)), dma((k_dp,)),
+        dma((k_mp, chunks)), dma((k_mp, chunks)), dma((k_mp, chunks)), dma((k_mp, chunks)),
+        dma((k_dp,)), dma((k_dp,)), dma((k_dp,)), dma((k_dp,)),
+        dma((hops,)), dma((hops,)),
+    ]
+    anywhere = pl.BlockSpec(memory_space=pl.ANY)
+    flops = 2 * rows * (depth_in * width_i + depth_out * width_o)
+    flops += 2 * tokens * width_i * width_o * (1 + queries // QTOK)
+    return pl.pallas_call(
+        functools.partial(kernel, (n_mp, n_dp, chunks)),
+        out_shape=(
+            jax.ShapeDtypeStruct((width_i, width_o), F32),
+            jax.ShapeDtypeStruct(small[1:], F32),
+        ),
+        in_specs=[anywhere] * 6,
+        out_specs=(anywhere, pl.BlockSpec(memory_space=pltpu.VMEM)),
+        scratch_shapes=scratch,
+        cost_estimate=pl.CostEstimate(
+            flops=flops,
+            bytes_accessed=2 * depth_out * width_o + 4 * width_i * width_o,
+            transcendentals=0,
+        ),
+        compiler_params=pltpu.CompilerParams(
+            collective_id=0, has_side_effects=True, vmem_limit_bytes=63 * 2**20
+        ),
+    )(acts, query_acts, grads, query_grads, basis_in, basis_out)
 
 
 def split_rows(joined, groups, first):
@@ -16,7 +428,7 @@
     return (shaped[:, :first].reshape(-1, width), shaped[:, first:].reshape(-1, width))
 
 
-def shards(acts, grads, query_acts, query_grads, basis_in, basis_out):
+def plain(acts, grads, query_acts, query_grads, basis_in, basis_out):
     n_model = lax.axis_size("mp")
     n_data = lax.axis_size("dp")
     rows_in = jnp.concatenate([acts, query_acts], axis=0)
@@ -56,8 +468,34 @@
         return (carry, jnp.sum(mapped * tok_out, axis=1))
 
     unused, partial_scores = lax.scan(one_query, jnp.zeros((), jnp.float32), (qa_blocks, qg_blocks))
-    scores = lax.psum(partial_scores, ("dp", "mp")) * math.sqrt(QTOK / (D * K))
+    scores = lax.psum(partial_scores, ("dp", "mp")) * math.sqrt(QTOK / (basis_in.shape[1] * n_model * basis_out.shape[1] * n_data))
     return (eigenvalues, scores)
+
+
+def shards(acts, grads, query_acts, query_grads, basis_in, basis_out):
+    n_mp, n_dp = lax.axis_size("mp"), lax.axis_size("dp")
+    width_i, width_o = basis_in.shape[1], basis_out.shape[1]
+    chunks = 7
+    owned = (acts.shape[0] + query_acts.shape[0]) * n_mp
+    aligned = (
+        n_mp == 2 ** log2(n_mp)
+        and n_dp == 2 ** log2(n_dp)
+        and k_fits(n_mp, n_dp)
+        and width_o % (chunks * 256) == 0
+        and width_i % 256 == 0
+        and owned % (16 * n_mp) == 0
+        and owned % (16 * n_dp) == 0
+        and all(a.shape[0] % 16 == 0 for a in (acts, query_acts, grads, query_grads))
+    )
+    if aligned:
+        return fused(
+            n_mp, n_dp, chunks, acts, grads, query_acts, query_grads, basis_in, basis_out
+        )
+    return plain(acts, grads, query_acts, query_grads, basis_in, basis_out)
+
+
+def k_fits(n_mp, n_dp):
+    return n_dp > 1 and log2(n_mp) > log2(n_dp)
 
 
 def solution(mesh):

time: 869 us -> 333 us (0.38)
  blocking collectives: 549 us -> 0 us
  Pallas kernels: 0 us -> 320 us
  matrix products: 219 us -> 0 us
  waiting for transfers between devices: 62.3 us -> 0 us
  between operations: 14.1 us -> 0.65 us
  other arithmetic: 9.89 us -> 0 us
    psum x3 -> x0, blocking collectives: 549 us -> none  [the longest x1 426 us: shards(): rot_out = lax.psum(part_out, 'mp').astype(jnp.bfloat16)]
    pallas_call x0 -> x1, Pallas kernels: none -> 320 us  [fused(): pl.pallas_call(functools.partial(kernel, (n_mp, n_dp, chunks)), out_shape...]
    dot_general x19 -> x0, matrix products: 219 us -> none  [the longest x16 172 us: one_query(): mapped = jnp.dot(tok_in, precond, preferred_element_type=jnp.float32)]
    all_gather x2 -> x0, waiting for transfers between devices: 62.3 us -> none  [the longest x1 62.2 us: shards(): lax.all_gather(rows_in, 'mp', axis=0, tiled=True)]
    unnamed x4, local copies, waits for them, and re-layouts: 0.01 us -> 12.3 us
  transfers between devices with their start and end apart: 2 -> 0, of which waited for: 1 -> 0; matrix products, arithmetic and copies ran while one was open for 1% -> 0% of each run, Pallas kernels for 0% -> 0%
where the time goes in v1:
time: 333 us
  Pallas kernels  320 us (96%)
  local copies, waits for them, and re-layouts  12.3 us (4%)
    pallas_call x1, Pallas kernels, fused(): pl.pallas_call(functools.partial(kernel, (n_mp, n_dp, chunks)), out_shape...  320 us
    unnamed x4, local copies, waits for them, and re-layouts  12.3 us

profile of v1, /device:TPU:0, one launch (start us, length us, event | category | flops | bytes accessed | tf_op | source)
XLA Modules:
  0.0 333.3 jit_solution(18075186749142219761)
XLA Ops:
  0.6 320.4 %shard_map.77 = (f32[1024,3584]{1,0:T(8,128)}, f32[16,512]{1,0:T(8,128)}) custom-call(bf16[64,2048]{1,0:T(8,128)(2,1)} %refs_0_.1, bf16[32,2048]{1,0:T(8,128)(2,1)} %refs_1_.1, bf16[128,3584]{1,0:T(8,128)(2,1)} %refs_2_.1, bf16[64,3584]{1,0:T(8,128)(2,1)} %refs_3_.1, bf16[2048,1024]{1,0:T(8,128)(2,1)} %refs_4_.1, bf16[3584,3584]{1,0:T(8,128)(2,1)} %refs_5_.1), custom_call_target="tpu_custom_call" | custom-call | flops 86838870016 | bytes 40370176 | tf_op jit(solution)/shard_map/pallas_call | solution.py:405
  321.0 0.0 copy-start
  321.0 11.6 %copy.10 = f32[1024,3584]{1,0:T(8,128)} copy(f32[1024,3584]{1,0:T(8,128)} %get-tuple-element.4) | data formatting | bytes 29360128
  332.7 0.0 copy-done
  332.7 0.6 copy.11
Async XLA Ops:
  321.0 11.6 %copy-start = (f32[16,512]{1,0:T(8,128)S(1)}, f32[16,512]{1,0:T(8,128)}, u32[]{:S(2)}) copy-start(f32[16,512]{1,0:T(8,128)} %get-tuple-element.5) | copy-start | bytes 98308

commit v2 on v1

--- a/solution.py
+++ b/solution.py
@@ -129,19 +129,33 @@
         irs_at.append(offset)
         offset += rows // 2 ** (s + 1)
 
+    def by_parity(c, even, odd):
+        return even + (c % 2) * (odd - even)
+
+    def bit_out(s, c):
+        return by_parity(c, bit(mp, s), bit(mp, (s + 1) % k_mp))
+
+    def peer_out(s, c):
+        step = by_parity(c, 2**s, 2 ** ((s + 1) % k_mp))
+        return (dp, mp + (1 - 2 * bit_out(s, c)) * step)
+
+    def start_out(c, step):
+        size = rows // 2**step
+        return sum(bit_out(b, c) * (rows // 2 ** (b + 1)) for b in range(step)), size
+
     def rs_copy(s, c):
         size = rows // 2 ** (s + 1)
         slot = pl.ds(rs_at[s], size)
         return remote(
-            send_rs.at[c, slot], recv_rs.at[c, slot], rs_s.at[s, c], rs_r.at[s, c], along_mp(s)
+            send_rs.at[c, slot], recv_rs.at[c, slot], rs_s.at[s, c], rs_r.at[s, c], peer_out(s, c)
         )
 
     def ag_copy(s, c):
-        start, size = split_start(mp, k_mp, k_mp - s)
+        start, size = start_out(c, k_mp - s)
         block = rows_at(start, size)
         return remote(
             rot_out.at[c, block], rot_out.at[c, block], ag_s.at[s, c], ag_r.at[s, c],
-            along_mp(k_mp - 1 - s),
+            peer_out(k_mp - 1 - s, c),
         )
 
     def irs_copy(s):
@@ -164,8 +178,8 @@
     def rotate_out(c):
         load_chunk(c).wait()
         slot, ring = lax.rem(c, 2), lax.rem(c, k_mp + 1)
-        theirs = rows_at((1 - bit(mp, 0)) * half, half)
-        mine = rows_at(bit(mp, 0) * half, half)
+        theirs = rows_at((1 - bit_out(0, c)) * half, half)
+        mine = rows_at(bit_out(0, c) * half, half)
         tile = 256
 
         @pl.loop(0, cw // tile)
@@ -190,18 +204,18 @@
     def reduce_out(s, c):
         rs_copy(s - 1, c).wait_recv()
         ring = lax.rem(c, k_mp + 1)
-        start, size = split_start(mp, k_mp, s)
-        start = start - bit(mp, 0) * half
+        start, size = start_out(c, s)
+        start = start - bit_out(0, c) * half
         if s == k_mp:
             total = acc[ring, rows_at(start, size), :] + recv_rs[
                 c, pl.ds(rs_at[s - 1], size), :
             ].astype(F32)
-            begin, _ = split_start(mp, k_mp, k_mp)
+            begin, _ = start_out(c, k_mp)
             rot_out[c, rows_at(begin, size), :] = total.astype(BF16)
             ag_copy(0, c).start()
             return
         part_size = size // 2
-        theirs, mine = (1 - bit(mp, s)) * part_size, bit(mp, s) * part_size
+        theirs, mine = (1 - bit_out(s, c)) * part_size, bit_out(s, c) * part_size
         base = rs_at[s - 1]
         send_rs[c, pl.ds(rs_at[s], part_size), :] = (
             acc[ring, rows_at(start + theirs, part_size), :]
@@ -290,18 +304,27 @@
 
         eig_copy(c).start()
 
-        @pl.loop(0, queries)
-        def _(q):
+        tall = math.gcd(width_i, 512)
+        group = math.gcd(queries, 2)
+
+        @pl.loop(0, queries // group)
+        def _(n):
             owner = lax.broadcasted_iota(jnp.int32, qgrad.shape, 0) // QTOK
-            right = jnp.where(owner == q, qgrad[...].astype(F32), 0.0).astype(BF16)
-            total = jnp.zeros((1, tokens), F32)
-            for i in range(width_i // ti):
-                at = pl.ds(i * ti, ti)
-                rotated = jnp.dot(qact_t[at, :], right, preferred_element_type=F32)
-                precond = (rotated * inverse[at, :]).astype(BF16)
-                mapped = jnp.dot(precond, grad_t[...], preferred_element_type=F32)
-                total = total + jnp.sum(mapped * act_t[at, :], axis=0, keepdims=True)
-            part[0, pl.ds(q, 1), :] = part[0, pl.ds(q, 1), :] + total
+            every = qgrad[...].astype(F32)
+            rights = [
+                jnp.where(owner == n * group + g, every, 0.0).astype(BF16) for g in range(group)
+            ]
+            totals = [jnp.zeros((1, tokens), F32)] * group
+            for i in range(width_i // tall):
+                at = pl.ds(i * tall, tall)
+                for g in range(group):
+                    rotated = jnp.dot(qact_t[at, :], rights[g], preferred_element_type=F32)
+                    precond = (rotated * inverse[at, :]).astype(BF16)
+                    mapped = jnp.dot(precond, grad_t[...], preferred_element_type=F32)
+                    totals[g] = totals[g] + jnp.sum(mapped * act_t[at, :], axis=0, keepdims=True)
+            for g in range(group):
+                row = pl.ds(n * group + g, 1)
+                part[0, row, :] = part[0, row, :] + totals[g]
 
     lag = 2 * k_mp
 

time: 333 us -> 298 us (0.89)
  Pallas kernels: 320 us -> 285 us
    pallas_call x1, Pallas kernels: 320 us -> 285 us  [fused(): pl.pallas_call(functools.partial(kernel, (n_mp, n_dp, chunks)), out_shape...]
where the time goes in v2:
time: 298 us; the launch traced here: 297 us
  Pallas kernels  285 us (96%)
  local copies, waits for them, and re-layouts  12.3 us (4%)
    pallas_call x1, Pallas kernels, fused(): pl.pallas_call(functools.partial(kernel, (n_mp, n_dp, chunks)), out_shape...  285 us
    unnamed x4, local copies, waits for them, and re-layouts  12.3 us

profile of v2, /device:TPU:0, one launch (start us, length us, event | category | flops | bytes accessed | tf_op | source)
XLA Modules:
  0.0 297.4 jit_solution(1317188332818199159)
XLA Ops:
  0.6 284.5 %shard_map.77 = (f32[1024,3584]{1,0:T(8,128)}, f32[16,512]{1,0:T(8,128)}) custom-call(bf16[64,2048]{1,0:T(8,128)(2,1)} %refs_0_.1, bf16[32,2048]{1,0:T(8,128)(2,1)} %refs_1_.1, bf16[128,3584]{1,0:T(8,128)(2,1)} %refs_2_.1, bf16[64,3584]{1,0:T(8,128)(2,1)} %refs_3_.1, bf16[2048,1024]{1,0:T(8,128)(2,1)} %refs_4_.1, bf16[3584,3584]{1,0:T(8,128)(2,1)} %refs_5_.1), custom_call_target="tpu_custom_call" | custom-call | flops 86838870016 | bytes 40370176 | tf_op jit(solution)/shard_map/pallas_call | solution.py:428
  285.2 0.0 copy-start
  285.2 11.6 %copy.10 = f32[1024,3584]{1,0:T(8,128)} copy(f32[1024,3584]{1,0:T(8,128)} %get-tuple-element.4) | data formatting | bytes 29360128
  296.8 0.0 copy-done
  296.8 0.6 copy.11
Async XLA Ops:
  285.2 11.6 %copy-start = (f32[16,512]{1,0:T(8,128)S(1)}, f32[16,512]{1,0:T(8,128)}, u32[]{:S(2)}) copy-start(f32[16,512]{1,0:T(8,128)} %get-tuple-element.5) | copy-start | bytes 98308
